TPU v7x, 256 devices: a whole 4x4x8 slice. The times are simulated.
256 devices in a mesh: grp: 8 (over y, core), rep: 32 (over x, z).
Axes of the slice: x: 4, y: 4, z: 8, core: 2. Of those that a mesh axis runs over, the one named last changes fastest.
Arguments:
- tokens: bfloat16 [8, 2048, 3072], P('grp', 'rep'), may hold values from -13 to 13
- upstream: bfloat16 [8, 2048, 12288], P('grp', None, 'rep'), may hold values from -0.86178639 to 0.86178639
- momentum: bfloat16 [3072, 12288], P(None, 'rep'), may hold values from -6 to 6
- worker_error: bfloat16 [8, 3072, 12288], P('grp', None, 'rep'), may hold values from -4 to 4
- server_error: float32 [3072, 12288], P('grp', 'rep'), may hold values from -4 to 4
Outputs:
- new_momentum: bfloat16 [3072, 12288], P(None, 'rep')
- new_worker_error: bfloat16 [8, 3072, 12288], P('grp', None, 'rep')
- new_server_error: float32 [3072, 12288], P('grp', 'rep')
All inputs are finite; a program needn't handle non-finite values.
Results may differ from a plain program's by a relative error of at most 0.011.
Values may be sent and summed in bfloat16 or wider, within the bound.
A program may use at most 128 MiB of HBM per device.

v0:
```python
import jax
import jax.numpy as jnp
from jax import lax
from jax.sharding import PartitionSpec as P

DECAY_RATE = 0.9
LINEAR_SPAN = 0.0625
EPSILON = 1e-06


def quantize(blocks):
    energy = jnp.mean(blocks * blocks, axis=(1, 2), keepdims=True)
    scales = jnp.sqrt(energy + EPSILON).astype(jnp.bfloat16)
    widened = lax.optimization_barrier(scales).astype(jnp.float32)
    levels = jnp.clip(blocks / (LINEAR_SPAN * widened), -1.0, 1.0).astype(jnp.bfloat16)
    decoded = widened * lax.optimization_barrier(levels).astype(jnp.float32)
    return (scales, levels, decoded)


def body(tokens, upstream, momentum, worker_error, server_error):
    groups = lax.axis_size("grp")
    upstream_rows = upstream[0]
    row_count, col_count = momentum.shape
    contract = (((0,), (0,)), ((), ()))
    inputs = lax.all_gather(tokens[0], "rep", axis=0, tiled=True)
    gradient = lax.dot_general(inputs, upstream_rows, contract, preferred_element_type=jnp.float32)
    buffer = (
        DECAY_RATE * momentum.astype(jnp.float32)
        + (1.0 - DECAY_RATE) * gradient
        + worker_error[0].astype(jnp.float32)
    )
    blocks = buffer.reshape(groups, row_count // groups, col_count)
    scales, levels, decoded = quantize(blocks)
    new_worker_error = (blocks - decoded).reshape(1, row_count, col_count).astype(jnp.bfloat16)
    got_levels, got_scales = (
        lax.all_to_all(levels, "grp", split_axis=0, concat_axis=0, tiled=True),
        lax.all_to_all(scales, "grp", split_axis=0, concat_axis=0, tiled=True),
    )
    summed = jnp.sum(got_scales.astype(jnp.float32) * got_levels.astype(jnp.float32), axis=0)
    average = summed / groups + server_error
    owner_scales, owner_levels, owner_decoded = quantize(average[None])
    new_server_error = average - owner_decoded[0]
    every_levels, every_scales = (
        lax.all_gather(owner_levels, "grp", axis=0, tiled=True),
        lax.all_gather(owner_scales, "grp", axis=0, tiled=True),
    )
    new_momentum = every_scales.astype(jnp.float32) * every_levels.astype(jnp.float32)
    new_momentum = new_momentum.reshape(row_count, col_count).astype(jnp.bfloat16)
    return (new_momentum, new_worker_error, new_server_error)


def solution(mesh):
    placed = (
        P("grp", "rep", None),
        P("grp", None, "rep"),
        P(None, "rep"),
        P("grp", None, "rep"),
        P("grp", "rep"),
    )
    return jax.shard_map(
        body,
        mesh=mesh,
        in_specs=placed,
        out_specs=(P(None, "rep"), P("grp", None, "rep"), P("grp", "rep")),
        check_vma=False,
    )
```

profile of v0, /device:TPU:1, one launch (start us, length us, event | category | flops | bytes accessed | tf_op | source)
XLA Modules:
  0.0 230.6 jit_solution(6892096601617969399)
XLA Ops:
  7.2 0.0 copy-start
  7.2 0.0 all-gather.5.cloned.1.call-start
  7.2 0.7 all-gather.5.cloned.1.call-update
  7.9 125.8 %all-gather.5.cloned.1.call-done = bf16[1,2048,3072]{2,1,0:T(8,128)(2,1)} async-done(((bf16[1,64,3072]{2,1,0:T(8,128)(2,1)}), bf16[1,2048,3072]{2,1,0:T(8,128)(2,1)}) %all-gather.5.cloned.1.call-update) | async-done | bytes 12582928 | tf_op jit(solution)/shard_map/all_gather | solution.py:25
  133.7 0.0 copy-done
  133.7 12.4 %multiply_reduce_fusion.1 = (f32[3072]{0:T(1024)S(1)}, f32[3072,384]{1,0:T(8,128)}) fusion(bf16[1,3072,384]{2,1,0:T(8,128)(2,1)} %param.8, bf16[1,2048,384]{2,1,0:T(8,128)(2,1)S(1)} %copy-done, bf16[1,2048,3072]{2,1,0:T(8,128)(2,1)} %all-gather.5.cloned.1.call-done, bf16[3072,384]{1,0:T(8,128)(2,1)} %param.7), kind=kOutput, calls=%fused_computation.8 | convolution fusion | flops 4841272320 | bytes 23605248 | tf_op jit(solution)/shard_map/dot_general | solution.py:26
  146.1 0.1 reduce_sum.36
  146.2 0.7 copy.10
  146.9 5.3 %all-to-all-start = ((bf16[8,1,1]{2,1,0:T(2,128)(2,1)}), bf16[8,1,1]{2,1,0:T(2,128)(2,1)S(1)}, u32[]{:S(2)}, u32[]{:S(2)}) async-start(bf16[8,1,1]{2,1,0:T(2,128)(2,1)} %copy.10), calls=%async_computation | async-start | bytes 8192 | tf_op jit(solution)/shard_map/all_to_all | solution.py:37
  152.2 4.3 %clamp_convert_fusion = bf16[8,384,384]{2,1,0:T(8,128)(2,1)} fusion(f32[8,384,384]{2,1,0:T(8,128)} %bitcast.34, f32[8]{0:T(128)S(1)} %multiply_bitcast_fusion), kind=kLoop, calls=%fused_computation.7 | loop fusion | flops 3538944 | bytes 7077920 | tf_op jit(solution)/shard_map/convert_element_type | solution.py:15
  156.5 0.0 copy-start.1
  156.5 0.0 copy-start.3
  156.5 0.2 all-to-all-done
  156.7 4.9 %all-to-all-start.1 = ((bf16[8,384,384]{2,1,0:T(8,128)(2,1)}), bf16[8,384,384]{2,1,0:T(8,128)(2,1)}, u32[]{:S(2)}, u32[]{:S(2)}) async-start(bf16[8,384,384]{2,1,0:T(8,128)(2,1)} %clamp_convert_fusion), calls=%async_computation.1 | async-start | bytes 4718592 | tf_op jit(solution)/shard_map/all_to_all | solution.py:36
  161.7 0.0 all-gather.7.cloned.1.call-start
  161.7 0.1 convert_reduce_fusion
  161.8 29.1 %all-to-all-done.1 = bf16[8,384,384]{2,1,0:T(8,128)(2,1)} async-done(((bf16[8,384,384]{2,1,0:T(8,128)(2,1)}), bf16[8,384,384]{2,1,0:T(8,128)(2,1)}, u32[]{:S(2)}, u32[]{:S(2)}) %all-to-all-start.1) | async-done | bytes 2359328 | tf_op jit(solution)/shard_map/all_to_all | solution.py:36
  190.9 2.3 multiply_reduce_fusion
  193.2 0.0 copy-done.1
  193.2 0.8 multiply_reduce_fusion.2
  194.7 0.8 clamp_convert_fusion.1
  195.5 0.0 all-gather.7.cloned.1.call-update
  195.5 0.0 copy-done.3
  195.5 0.6 dynamic-slice
  196.1 0.7 dynamic-update-slice
  196.8 0.0 copy-start.2
  196.8 5.3 %subtract_convert_fusion = bf16[8,384,384]{2,1,0:T(8,128)(2,1)} fusion(f32[8,384,384]{2,1,0:T(8,128)} %bitcast.35, bf16[8,384,384]{2,1,0:T(8,128)(2,1)} %clamp_convert_fusion, f32[8]{0:T(128)S(1)} %convert_bitcast_fusion), kind=kLoop, calls=%fused_computation.5 | loop fusion | flops 4718592 | bytes 9437216 | tf_op jit(solution)/shard_map/convert_element_type | solution.py:34
  202.1 12.6 %all-reduce = bf16[8]{0:T(256)(128)(2,1)S(1)} all-reduce(bf16[8]{0:T(256)(128)(2,1)S(1)} %dynamic-update-slice), channel_id=1, replica_groups=mesh['grp'=8,'rep'=32] {'grp'}, use_global_device_ids=true, to_apply=%add | all-reduce | flops 8 | bytes 32
  214.7 0.0 copy-done.2
  214.7 0.9 bitcast_subtract_fusion
  215.7 4.2 %all-gather.7.cloned.1.call-done = bf16[3072,384]{1,0:T(8,128)(2,1)} async-done(((bf16[384,384]{1,0:T(8,128)(2,1)}), bf16[3072,384]{1,0:T(8,128)(2,1)}) %all-gather.7.cloned.1.call-update) | async-done | bytes 2359312 | tf_op jit(solution)/shard_map/all_gather | solution.py:44
  219.9 3.9 %fusion.2 = bf16[8,384,384]{2,1,0:T(8,128)(2,1)} fusion(bf16[8,384,384]{2,1,0:T(8,128)(2,1)} %bitcast.37, f32[8]{0:T(128)S(1)} %mul.96), kind=kLoop, calls=%fused_computation.3 | loop fusion | flops 3538944 | bytes 4718624 | tf_op jit(solution)/shard_map/convert_element_type | solution.py:48
  (6 shorter events, 0.0 us)
Async XLA Ops:
  7.2 126.5 %copy-start = (bf16[1,2048,384]{2,1,0:T(8,128)(2,1)S(1)}, bf16[1,2048,384]{2,1,0:T(8,128)(2,1)}, u32[]{:S(2)}) copy-start(bf16[1,2048,384]{2,1,0:T(8,128)(2,1)} %param.6) | copy-start | bytes 4718596
  7.2 126.5 %all-gather.5.cloned.1.call-start = ((), (), s32[]{:S(2)}) async-start(), calls=%async_computation.2 | async-start | bytes 12976128 | tf_op jit(solution)/shard_map/all_gather | solution.py:25
  146.9 9.8 %all-to-all-start = ((bf16[8,1,1]{2,1,0:T(2,128)(2,1)}), bf16[8,1,1]{2,1,0:T(2,128)(2,1)S(1)}, u32[]{:S(2)}, u32[]{:S(2)}) async-start(bf16[8,1,1]{2,1,0:T(2,128)(2,1)} %copy.10), calls=%async_computation | async-start | bytes 8192 | tf_op jit(solution)/shard_map/all_to_all | solution.py:37
  156.5 36.7 %copy-start.1 = (f32[384,384]{1,0:T(8,128)S(1)}, f32[384,384]{1,0:T(8,128)}, u32[]{:S(2)}) copy-start(f32[384,384]{1,0:T(8,128)} %param.9) | copy-start | bytes 1769476
  156.5 39.1 %copy-start.3 = (u32[256]{0:T(256)S(1)}, u32[256]{0:T(256)}, u32[]{:S(2)}) copy-start(u32[256]{0:T(256)} %constant.32) | copy-start | bytes 3076
  156.7 34.2 %all-to-all-start.1 = ((bf16[8,384,384]{2,1,0:T(8,128)(2,1)}), bf16[8,384,384]{2,1,0:T(8,128)(2,1)}, u32[]{:S(2)}, u32[]{:S(2)}) async-start(bf16[8,384,384]{2,1,0:T(8,128)(2,1)} %clamp_convert_fusion), calls=%async_computation.1 | async-start | bytes 4718592 | tf_op jit(solution)/shard_map/all_to_all | solution.py:36
  161.7 58.2 %all-gather.7.cloned.1.call-start = ((), (), s32[]{:S(2)}) async-start(), calls=%async_computation.3 | async-start | bytes 2654208 | tf_op jit(solution)/shard_map/all_gather | solution.py:44
  196.8 17.9 %copy-start.2 = (bf16[384,384]{1,0:T(8,128)(2,1)S(1)}, bf16[384,384]{1,0:T(8,128)(2,1)}, u32[]{:S(2)}) copy-start(bf16[384,384]{1,0:T(8,128)(2,1)} %clamp_convert_fusion.1) | copy-start | bytes 884740
Sparse Core Ops, SparseCore 0:
  10.6 123.0 all-gather.4
  195.7 24.1 all-gather.6
where the time goes:
time: 231 us
  waiting for transfers between devices  160 us (69%)
  other arithmetic  18.5 us (8%)
  between operations  14.8 us (6%)
  blocking collectives  12.6 us (5%)
  matrix products  12.4 us (5%)
  starting transfers between devices  10.3 us (4%)
    all_gather x1, waiting for transfers between devices, body(): inputs = lax.all_gather(tokens[0], 'rep', axis=0, tiled=True)  126 us
    all_to_all x1, waiting for transfers between devices, body(): lax.all_to_all(levels, 'grp', split_axis=0, concat_axis=0, tiled=True)  29.1 us
    unnamed x1, blocking collectives  12.6 us
    dot_general x1, matrix products, body(): lax.dot_general(inputs, upstream_rows, contract, preferred_element_type=j...  12.4 us
    all_to_all x1, starting transfers between devices, body(): lax.all_to_all(scales, 'grp', split_axis=0, concat_axis=0, tiled=True)  5.33 us
    convert_element_type x1, other arithmetic, body(): (blocks - decoded).reshape(1, row_count, col_count).astype(jnp.bfloat16)  5.29 us
    convert_element_type x2, other arithmetic, quantize(): jnp.clip(blocks / (LINEAR_SPAN * widened), -1.0, 1.0).astype(jnp.bfloat16)  5.1 us
    all_to_all x1, starting transfers between devices, body(): lax.all_to_all(levels, 'grp', split_axis=0, concat_axis=0, tiled=True)  4.94 us
  transfers between devices with their start and end apart: 4, of which 4 were waited for; matrix products, arithmetic and copies ran while one was open for 5% of the time, Pallas kernels for 0%

commit v1 on v0

v1 whole, which is shorter than its diff:
```python
import functools

import jax
import jax.numpy as jnp
from jax import lax
from jax.experimental import pallas as pl
from jax.experimental.pallas import tpu as pltpu
from jax.sharding import PartitionSpec as P

DECAY_RATE = 0.9
LINEAR_SPAN = 0.0625
EPSILON = 1e-06
MESH = pl.DeviceIdType.MESH

NX, NY, NZ = 4, 4, 8
GROUPS = 8
ROWS = 64
SIDE = 384
PIECE = 128
PIECES = 12
HEAD = 16
STEP = 32
HALF = SIDE // 2

FIRST_MM = 9
RELAY = 8


def done_pieces(tick):
    return max(0, min(2 * (tick - FIRST_MM + 1), tick - 4, PIECES))


def done_stretches(tick):
    return (2 * done_pieces(tick - 1)) // 3


def first_tick(predicate):
    return next(tick for tick in range(100) if predicate(tick))


OWN_0 = first_tick(lambda t: done_stretches(t - 1) >= 4)
OWN_1 = first_tick(lambda t: done_stretches(t - 1) >= 8)
TICKS = OWN_1 + 4


def traced_pieces(tick):
    return jnp.maximum(0, jnp.minimum(jnp.minimum(2 * (tick - FIRST_MM + 1), tick - 4), PIECES))


def traced_stretches(tick):
    return (2 * traced_pieces(tick - 1)) // 3


def stretch_of(y, core, c):
    hop = c + 1
    forward = lax.rem(y + hop, 4)
    backward = lax.rem(y + 3 * hop, 4)
    return 2 * jnp.where(core == 0, forward, backward) + c // 4


def kernel(
    tok_ref, up_ref, mom_ref, we_ref, se_ref,
    nm_out, nwe_out, nse_out,
    tok_a, tok_b, up_a, up_b, grads, sent_own, sent_far, mom, we, nwe, lev, got, nm, se, work, nse,
    s_in, s_send, s_dist, s_ax, s_az, s_bx, s_bz, s_up, s_far, s_relay, s_grad, s_lev, s_nm, s_half, s_out,
):
    grp = lax.axis_index("grp")
    rep = lax.axis_index("rep")
    y, j = grp // 2, lax.rem(grp, 2)
    x, z = rep // NZ, lax.rem(rep, NZ)
    h = x // 2
    q = lax.rem((x + 1) // 2, 2)
    x_in = x + 1 - 2 * lax.rem(x, 2)
    x_far = 3 - x
    z_up, z_down = lax.rem(z + 1, NZ), lax.rem(z + NZ - 1, NZ)
    y_up, y_down = lax.rem(y + 1, NY), lax.rem(y + NY - 1, NY)
    home = j == h

    def device(xx, yy, zz, core):
        return (2 * yy + core, NZ * xx + zz)

    inner = device(x_in, y, z, j)
    above = device(x, y, z_up, j)
    below = device(x, y, z_down, j)
    sibling = device(x, y, z, 1 - j)

    def remote(src, dst, sem, target):
        pltpu.make_async_remote_copy(
            src_ref=src, dst_ref=dst, send_sem=s_send, recv_sem=sem, device_id=target, device_id_type=MESH
        ).start()

    def local(src, dst, sem):
        pltpu.make_async_copy(src, dst, sem).start()

    def wait(ref, sem):
        pltpu.make_async_copy(ref, ref, sem).wait()

    barrier = pltpu.get_barrier_semaphore()
    greeted = [inner, above, below, device(x_far, y, z, 0), device(x_far, y, z, 1), sibling]
    for hop in range(1, NY):
        for core in range(2):
            greeted.append(device(x, lax.rem(y + hop, NY), z, core))
    for target in greeted:
        pl.semaphore_signal(barrier, inc=1, device_id=target, device_id_type=MESH)
    pl.semaphore_wait(barrier, len(greeted))

    near_x = jnp.where(home, x, x_far)

    def distribute(i, carry):
        for core in range(2):
            piece = 2 * i + core
            column = stretch_of(y, j, piece // 3) * SIDE + lax.rem(piece, 3) * PIECE
            src = tok_ref.at[:, pl.ds(pl.multiple_of(column, PIECE), PIECE)]
            for half in range(2):
                dst = tok_a.at[i, z, q] if half == 0 else tok_b.at[i, q, z]
                sem = s_dist.at[i, half]
                if core == half:

                    @pl.when((h == half) & home)
                    def _():
                        local(src, dst, sem)

                    @pl.when((h == half) & jnp.logical_not(home))
                    def _():
                        remote(src, dst, sem, device(x_far, y, z, core))
                else:

                    @pl.when(h == half)
                    def _():
                        remote(src, dst, sem, device(near_x, y, z, core))

        return carry

    lax.fori_loop(0, PIECES, distribute, 0)

    @pl.when(home)
    def _():
        for k in range(2):
            local(up_ref.at[k], up_a.at[0, :, k], s_up.at[k])
            local(up_ref.at[3 - k], up_b.at[0, k], s_up.at[2 + k])
        for k in range(2):
            remote(up_ref.at[k], up_a.at[0, :, k], s_up.at[k], sibling)
            remote(up_ref.at[3 - k], up_b.at[0, k], s_up.at[2 + k], sibling)

    @pl.when(jnp.logical_not(home))
    def _():
        for k in range(2):
            remote(up_ref.at[k], up_a.at[1, :, k], s_far.at[0], device(x_far, y, z, k))
            remote(up_ref.at[3 - k], up_b.at[1, k], s_far.at[1], device(x_far, y, z, k))

    local(mom_ref, mom, s_in.at[0])
    local(we_ref, we, s_in.at[1])
    local(se_ref, se, s_in.at[2])

    z_at = lambda d: lax.rem(z + d + NZ, NZ)

    def matmul(i, carry):
        left_a = tok_a[i].reshape(16 * ROWS, PIECE)
        left_b = tok_b[i].reshape(16 * ROWS, PIECE)
        contract = (((0,), (0,)), ((), ()))
        piece = 2 * i + j

        def product(slot):
            one = lax.dot_general(left_a, up_a[slot].reshape(16 * ROWS, SIDE), contract, preferred_element_type=jnp.float32)
            two = lax.dot_general(left_b, up_b[slot].reshape(16 * ROWS, SIDE), contract, preferred_element_type=jnp.float32)
            return (one + two).astype(jnp.bfloat16)

        sent_far[i] = product(1)
        remote(sent_far.at[i], grads.at[piece], s_grad.at[piece], device(x_far, y, z, h))
        own = product(0)

        @pl.when(home)
        def _():
            grads[piece] = own

        @pl.when(jnp.logical_not(home))
        def _():
            sent_own[i] = own
            remote(sent_own.at[i], grads.at[piece], s_grad.at[piece], sibling)

        return carry

    def scale_of(total):
        energy = jnp.sum(jnp.sum(total, axis=0, keepdims=True), axis=1, keepdims=True) * (1.0 / (SIDE * SIDE))
        scale = jnp.sqrt(energy + EPSILON).astype(jnp.bfloat16)
        return scale, scale.astype(jnp.float32)

    def compress(c, carry):
        at = stretch_of(y, j, c)
        total = jnp.zeros((STEP, SIDE), jnp.float32)
        for m in range(3):
            piece = 3 * c + m

            @pl.when(jnp.logical_not(home & (lax.rem(piece, 2) == j)))
            def _():
                wait(grads.at[piece], s_grad.at[piece])

            def add(n, total, m=m, piece=piece):
                row = n * STEP
                rows = pl.ds(pl.multiple_of(m * PIECE + row, STEP), STEP)
                value = (
                    DECAY_RATE * mom[at, rows].astype(jnp.float32)
                    + (1.0 - DECAY_RATE) * grads[piece, pl.ds(pl.multiple_of(row, STEP), STEP)].astype(jnp.float32)
                    + we[at, rows].astype(jnp.float32)
                )
                work[rows] = value
                return total + value * value

            total = lax.fori_loop(0, PIECE // STEP, add, total)
        scale, wide = scale_of(total)
        inverse = 1.0 / (LINEAR_SPAN * wide)
        lev[c, pl.ds(SIDE, HEAD)] = jnp.broadcast_to(scale, (HEAD, SIDE))

        def code(n, carry):
            rows = pl.ds(pl.multiple_of(n * STEP, STEP), STEP)
            value = work[rows]
            level = jnp.clip(value * inverse, -1.0, 1.0).astype(jnp.bfloat16)
            lev[c, rows] = level
            nwe[c, rows] = (value - wide * level.astype(jnp.float32)).astype(jnp.bfloat16)
            return carry

        lax.fori_loop(0, SIDE // STEP, code, 0)
        mine = at == grp

        @pl.when(mine)
        def _():
            local(lev.at[c], got.at[grp], s_lev.at[grp])

        @pl.when(jnp.logical_not(mine))
        def _():
            remote(lev.at[c], got.at[grp], s_lev.at[grp], (at, rep))

        local(nwe.at[c], nwe_out.at[at], s_out.at[0])
        return carry

    def own():
        for k in range(GROUPS):
            wait(got.at[k], s_lev.at[k])
        scales = [got[k, pl.ds(SIDE, HEAD)][0:1].astype(jnp.float32) for k in range(GROUPS)]

        def add(n, total):
            rows = pl.ds(pl.multiple_of(n * STEP, STEP), STEP)
            value = scales[0] * got[0, rows].astype(jnp.float32)
            for k in range(1, GROUPS):
                value += scales[k] * got[k, rows].astype(jnp.float32)
            value = value * (1.0 / GROUPS) + se[rows]
            work[rows] = value
            return total + value * value

        total = lax.fori_loop(0, SIDE // STEP, add, jnp.zeros((STEP, SIDE), jnp.float32))
        scale, wide = scale_of(total)
        inverse = 1.0 / (LINEAR_SPAN * wide)

        def code(n, carry):
            rows = pl.ds(pl.multiple_of(n * STEP, STEP), STEP)
            value = work[rows]
            level = jnp.clip(value * inverse, -1.0, 1.0).astype(jnp.bfloat16)
            decoded = wide * level.astype(jnp.float32)
            nm[grp, rows] = decoded.astype(jnp.bfloat16)
            nse[rows] = value - decoded
            return carry

        lax.fori_loop(0, SIDE // STEP, code, 0)
        block = nm.at[grp]
        remote(block, block, s_nm.at[grp], device(x, y_up, z, j))
        remote(block, block, s_nm.at[grp], device(x, y_down, z, j))
        remote(block, block, s_nm.at[grp], sibling)
        local(block, nm_out.at[grp], s_out.at[1])
        local(nse, nse_out, s_out.at[2])

    def spread_near():
        top, bottom = pl.ds(0, HALF), pl.ds(HALF, HALF)
        for yy, target, rows, which in ((y_down, y_up, top, 0), (y_up, y_down, bottom, 1)):
            at = 2 * yy + j
            wait(nm.at[at], s_nm.at[at])
            remote(nm.at[at, rows], nm.at[at, rows], s_half.at[which], device(x, target, z, j))
            remote(nm.at[at], nm.at[at], s_nm.at[at], sibling)
            local(nm.at[at], nm_out.at[at], s_out.at[1])

    def spread_far():
        at = 2 * lax.rem(y + 2, NY) + j
        wait(nm.at[at, pl.ds(0, HALF)], s_half.at[0])
        wait(nm.at[at, pl.ds(HALF, HALF)], s_half.at[1])
        remote(nm.at[at], nm.at[at], s_nm.at[at], sibling)
        local(nm.at[at], nm_out.at[at], s_out.at[1])

    def take(core):
        for hop in (0, 1, 3, 2):
            at = 2 * lax.rem(y + hop, NY) + core
            wait(nm.at[at], s_nm.at[at])
            local(nm.at[at], nm_out.at[at], s_out.at[1])

    def tick(t, carry):
        def stage(s):
            i = t - s
            return i, (i >= 0) & (i < PIECES)

        i0, on = stage(0)

        @pl.when(on)
        def _():
            i = i0
            wait(tok_a.at[i, z, q], s_dist.at[i, 0])
            block = tok_a.at[i, z, q]
            remote(block, block, s_ax.at[i], inner)
            wait(tok_b.at[i, q, z], s_dist.at[i, 1])
            block = tok_b.at[i, q, z]
            remote(block, block, s_bz.at[i, 0, 0], above)
            remote(block, block, s_bz.at[i, 0, 1], below)
            remote(block, block, s_bx.at[i], inner)

        for s in range(1, 6):
            i_s, on = stage(s)

            @pl.when(on)
            def _(i=i_s, s=s):
                if s == 1:
                    wait(tok_a.at[i, z, 1 - q], s_ax.at[i])
                    block = tok_a.at[i, z]
                    remote(block, block, s_az.at[i, 0, 0], above)
                    remote(block, block, s_az.at[i, 0, 1], below)
                elif s <= 3:
                    for way, sign, target in ((0, -1, above), (1, 1, below)):
                        block = tok_a.at[i, z_at(sign * (s - 1))]
                        wait(block, s_az.at[i, s - 2, way])
                        remote(block, block, s_az.at[i, s - 1, way], target)
                elif s == 4:
                    for way, sign, target in ((0, -1, above), (1, 1, below)):
                        block = tok_a.at[i, z_at(sign * 3)]
                        wait(block, s_az.at[i, 2, way])
                        part = tok_a.at[i, z_at(sign * 3), way]
                        remote(part, part, s_az.at[i, 3, way], target)
                else:
                    for way in range(2):
                        wait(tok_a.at[i, z_at(4), way], s_az.at[i, 3, way])
                if s <= 2:
                    for way, sign, target in ((0, -1, above), (1, 1, below)):
                        block = tok_b.at[i, q, z_at(sign * s)]
                        wait(block, s_bz.at[i, s - 1, way])
                        remote(block, block, s_bz.at[i, s, way], target)
                        remote(block, block, s_bx.at[i], inner)
                elif s == 3:
                    for way, sign, target in ((0, -1, above), (1, 1, below)):
                        block = tok_b.at[i, q, z_at(sign * 3)]
                        wait(block, s_bz.at[i, 2, way])
                        part = tok_b.at[i, q, z_at(sign * 3), pl.ds(32 * way, 32)]
                        remote(part, part, s_bz.at[i, 3, way], target)
                        remote(block, block, s_bx.at[i], inner)
                elif s == 4:
                    for way in range(2):
                        wait(tok_b.at[i, q, z_at(4), pl.ds(32 * way, 32)], s_bz.at[i, 3, way])
                    block = tok_b.at[i, q, z_at(4)]
                    remote(block, block, s_bx.at[i], inner)
                else:
                    wait(tok_b.at[i, 1 - q], s_bx.at[i])

        @pl.when(t == RELAY)
        def _():
            block = up_a.at[1, :, j]
            wait(block, s_far.at[0])
            remote(block, block, s_relay.at[0], sibling)
            block = up_b.at[1, j]
            wait(block, s_far.at[1])
            remote(block, block, s_relay.at[1], sibling)

        @pl.when(t == FIRST_MM)
        def _():
            for k in range(2):
                wait(up_a.at[0, :, k], s_up.at[k])
                wait(up_b.at[0, k], s_up.at[2 + k])
            wait(up_a.at[1, :, 1 - j], s_relay.at[0])
            wait(up_b.at[1, 1 - j], s_relay.at[1])
            wait(mom, s_in.at[0])
            wait(we, s_in.at[1])
            wait(se, s_in.at[2])

        lax.fori_loop(traced_pieces(t - 1), traced_pieces(t), matmul, 0)
        lax.fori_loop(traced_stretches(t - 1), traced_stretches(t), compress, 0)

        pl.when(t == jnp.where(j == 0, OWN_0, OWN_1))(own)
        pl.when(t == jnp.where(j == 0, OWN_0, OWN_1) + 1)(spread_near)
        pl.when(t == jnp.where(j == 0, OWN_0, OWN_1) + 2)(spread_far)

        @pl.when(t == jnp.where(j == 0, OWN_1, OWN_0) + 3)
        def _():
            take(1 - j)

        return carry

    lax.fori_loop(0, TICKS, tick, 0)

    for i in range(PIECES):
        pass

    def drain(i, carry):
        wait(tok_a.at[i], s_send)
        wait(tok_b.at[i, 0], s_send)
        wait(tok_b.at[i, 1, pl.ds(0, 6)], s_send)
        wait(sent_far.at[i], s_send)

        @pl.when(jnp.logical_not(home))
        def _():
            wait(sent_own.at[i], s_send)
            wait(tok_a.at[i, 0], s_send)

        @pl.when(home)
        def _():
            wait(tok_a.at[i, 0, 0], s_send)

        return carry

    lax.fori_loop(0, PIECES, drain, 0)
    wait(up_ref, s_send)
    wait(up_a.at[1, :, 0], s_send)
    wait(up_b.at[1, 0], s_send)

    def drain_levels(c, carry):
        @pl.when(stretch_of(y, j, c) != grp)
        def _():
            wait(lev.at[c], s_send)

        return carry

    lax.fori_loop(0, GROUPS, drain_levels, 0)
    for _ in range(7):
        wait(nm.at[0], s_send)
    wait(nwe, s_out.at[0])
    wait(nm, s_out.at[1])
    wait(nse, s_out.at[2])


def body(tokens, upstream, momentum, worker_error, server_error):
    bf16, f32 = jnp.bfloat16, jnp.float32
    anywhere = pl.BlockSpec(memory_space=pl.ANY)
    dma = pltpu.SemaphoreType.DMA
    stretches = (GROUPS, SIDE, SIDE)
    new_momentum, new_worker_error, new_server_error = pl.pallas_call(
        kernel,
        out_shape=(
            jax.ShapeDtypeStruct(stretches, bf16),
            jax.ShapeDtypeStruct(stretches, bf16),
            jax.ShapeDtypeStruct((SIDE, SIDE), f32),
        ),
        in_specs=[anywhere] * 5,
        out_specs=[anywhere] * 3,
        scratch_shapes=[
            pltpu.VMEM((PIECES, NZ, 2, ROWS, PIECE), bf16),
            pltpu.VMEM((PIECES, 2, NZ, ROWS, PIECE), bf16),
            pltpu.VMEM((2, NZ, 2, ROWS, SIDE), bf16),
            pltpu.VMEM((2, 2, NZ, ROWS, SIDE), bf16),
            pltpu.VMEM((2 * PIECES, PIECE, SIDE), bf16),
            pltpu.VMEM((PIECES, PIECE, SIDE), bf16),
            pltpu.VMEM((PIECES, PIECE, SIDE), bf16),
            pltpu.VMEM(stretches, bf16),
            pltpu.VMEM(stretches, bf16),
            pltpu.VMEM(stretches, bf16),
            pltpu.VMEM((GROUPS, SIDE + HEAD, SIDE), bf16),
            pltpu.VMEM((GROUPS, SIDE + HEAD, SIDE), bf16),
            pltpu.VMEM(stretches, bf16),
            pltpu.VMEM((SIDE, SIDE), f32),
            pltpu.VMEM((SIDE, SIDE), f32),
            pltpu.VMEM((SIDE, SIDE), f32),
            dma((3,)),
            dma,
            dma((PIECES, 2)),
            dma((PIECES,)),
            dma((PIECES, 4, 2)),
            dma((PIECES,)),
            dma((PIECES, 4, 2)),
            dma((4,)),
            dma((2,)),
            dma((2,)),
            dma((2 * PIECES,)),
            dma((GROUPS,)),
            dma((GROUPS,)),
            dma((2,)),
            dma((3,)),
        ],
        name="compressed_step",
        compiler_params=pltpu.CompilerParams(
            collective_id=0, has_side_effects=True, vmem_limit_bytes=48 * 1024 * 1024
        ),
    )(
        tokens[0],
        upstream[0].reshape(NX, NZ, ROWS, SIDE),
        momentum.reshape(stretches),
        worker_error[0].reshape(stretches),
        server_error,
    )
    return (
        new_momentum.reshape(GROUPS * SIDE, SIDE),
        new_worker_error.reshape(1, GROUPS * SIDE, SIDE),
        new_server_error,
    )


def solution(mesh):
    placed = (
        P("grp", "rep", None),
        P("grp", None, "rep"),
        P(None, "rep"),
        P("grp", None, "rep"),
        P("grp", "rep"),
    )
    return jax.shard_map(
        body,
        mesh=mesh,
        in_specs=placed,
        out_specs=(P(None, "rep"), P("grp", None, "rep"), P("grp", "rep")),
        check_vma=False,
    )
```

time: 231 us -> 113 us (0.49)
  waiting for transfers between devices: 160 us -> 0 us
  Pallas kernels: 0 us -> 104 us
  other arithmetic: 18.5 us -> 0 us
  between operations: 14.8 us -> 0.66 us
  blocking collectives: 12.6 us -> 0 us
  matrix products: 12.4 us -> 0 us
  starting transfers between devices: 10.3 us -> 0 us
  local copies, waits for them, and re-layouts: 1.97 us -> 8.19 us
    all_gather x2 -> x0, waiting for transfers between devices: 130 us -> none  [the longest x1 126 us: body(): inputs = lax.all_gather(tokens[0], 'rep', axis=0, tiled=True)]
    pallas_call x0 -> x1, Pallas kernels: none -> 104 us  [body(): pl.pallas_call(kernel, out_shape=(jax.ShapeDtypeStruct(stretches, bf16),...]
    all_to_all x2 -> x0, waiting for transfers between devices: 29.4 us -> none  [the longest x1 29.1 us: body(): lax.all_to_all(levels, 'grp', split_axis=0, concat_axis=0, tiled=True)]
    convert_element_type x5 -> x0, other arithmetic: 14.3 us -> none  [the longest x1 5.29 us: body(): (blocks - decoded).reshape(1, row_count, col_count).astype(jnp.bfloat16)]
    unnamed x1 -> x0, blocking collectives: 12.6 us -> none
    dot_general x1 -> x0, matrix products: 12.4 us -> none  [body(): lax.dot_general(inputs, upstream_rows, contract, preferred_element_type=j...]
    all_to_all x2 -> x0, starting transfers between devices: 10.3 us -> none  [the longest x1 5.33 us: body(): lax.all_to_all(scales, 'grp', split_axis=0, concat_axis=0, tiled=True)]
    unnamed x11, local copies, waits for them, and re-layouts: 1.27 us -> 8.19 us
  transfers between devices with their start and end apart: 4 -> 0, of which waited for: 4 -> 0; matrix products, arithmetic and copies ran while one was open for 5% -> 0% of each run, Pallas kernels for 0% -> 0%
where the time goes in v1:
time: 113 us
  Pallas kernels  104 us (92%)
  local copies, waits for them, and re-layouts  8.19 us (7%)
    pallas_call x1, Pallas kernels, body(): pl.pallas_call(kernel, out_shape=(jax.ShapeDtypeStruct(stretches, bf16),...  104 us
    unnamed x11, local copies, waits for them, and re-layouts  8.19 us

profile of v1, /device:TPU:1, one launch (start us, length us, event | category | flops | bytes accessed | tf_op | source)
XLA Modules:
  0.0 113.0 jit_solution(14866707931388227410)
XLA Ops:
  0.6 0.0 copy-start
  0.6 1.4 %copy-done = bf16[1,2048,384]{2,1,0:T(8,128)(2,1)S(1)} copy-done((bf16[1,2048,384]{2,1,0:T(8,128)(2,1)S(1)}, bf16[1,2048,384]{2,1,0:T(8,128)(2,1)}, u32[]{:S(2)}) %copy-start) | copy-done | bytes 1572888
  2.0 0.0 copy-start.1
  2.0 1.1 copy-done.1
  3.1 0.0 copy-start.2
  3.1 1.0 copy-done.2
  4.1 104.2 %compressed_step.1 = (bf16[8,384,384]{2,1,0:T(8,128)(2,1)S(1)}, bf16[8,384,384]{2,1,0:T(8,128)(2,1)}, f32[384,384]{1,0:T(8,128)S(1)}) custom-call(bf16[64,3072]{1,0:T(8,128)(2,1)S(1)} %bitcast.8, bf16[4,8,64,384]{3,2,1,0:T(8,128)(2,1)S(1)} %bitcast.7, bf16[8,384,384]{2,1,0:T(8,128)(2,1)} %bitcast.9, bf16[8,384,384]{2,1,0:T(8,128)(2,1)} %bitcast.10, ...), custom_call_target="tpu_custom_call" | custom-call | tf_op jit(solution)/shard_map/compressed_step/pallas_call | solution.py:437
  108.3 0.0 copy-start.3
  108.3 1.4 %copy.11 = bf16[3072,384]{1,0:T(8,128)(2,1)} copy(bf16[3072,384]{1,0:T(8,128)(2,1)S(1)} %bitcast.6) | data formatting | bytes 4718592
  109.7 1.1 copy-done.3
  110.8 1.4 %copy.12 = bf16[1,3072,384]{2,1,0:T(8,128)(2,1)} copy(bf16[1,3072,384]{2,1,0:T(8,128)(2,1)S(1)} %bitcast.11) | data formatting | bytes 4718592
  112.2 0.8 copy.13
Async XLA Ops:
  0.6 1.4 %copy-start = (bf16[1,2048,384]{2,1,0:T(8,128)(2,1)S(1)}, bf16[1,2048,384]{2,1,0:T(8,128)(2,1)}, u32[]{:S(2)}) copy-start(bf16[1,2048,384]{2,1,0:T(8,128)(2,1)} %param.6) | copy-start | bytes 4718596
  2.0 1.1 copy-start.1
  3.1 1.0 copy-start.2
  108.3 2.5 %copy-start.3 = (bf16[8,384,384]{2,1,0:T(8,128)(2,1)S(1)}, bf16[8,384,384]{2,1,0:T(8,128)(2,1)}, u32[]{:S(2)}) copy-start(bf16[8,384,384]{2,1,0:T(8,128)(2,1)} %get-tuple-element.7) | copy-start | bytes 7077892

commit v2 on v1

--- a/solution.py
+++ b/solution.py
@@ -22,40 +22,36 @@
 STEP = 32
 HALF = SIDE // 2
 
-FIRST_MM = 9
-RELAY = 8
+AHEAD = 1
+FIRST_MM = 7
+RELAY = 6
+LAG = 2
+LATE = 16
+OWN = (16, 17)
+NEAR = (17, 18)
+FAR = (18, 19)
+TAKE = (19, 20)
+TICKS = 21
+DRAIN = 17
+EARLY = 7
+
+
+def entered(tick):
+    return jnp.where(tick < 0, 0, jnp.minimum(tick + 1 + AHEAD, PIECES))
 
 
 def done_pieces(tick):
-    return max(0, min(2 * (tick - FIRST_MM + 1), tick - 4, PIECES))
+    return jnp.maximum(0, jnp.minimum(2 * (tick - FIRST_MM + 1), entered(tick - 5)))
 
 
 def done_stretches(tick):
-    return (2 * done_pieces(tick - 1)) // 3
-
-
-def first_tick(predicate):
-    return next(tick for tick in range(100) if predicate(tick))
-
-
-OWN_0 = first_tick(lambda t: done_stretches(t - 1) >= 4)
-OWN_1 = first_tick(lambda t: done_stretches(t - 1) >= 8)
-TICKS = OWN_1 + 4
-
-
-def traced_pieces(tick):
-    return jnp.maximum(0, jnp.minimum(jnp.minimum(2 * (tick - FIRST_MM + 1), tick - 4), PIECES))
-
-
-def traced_stretches(tick):
-    return (2 * traced_pieces(tick - 1)) // 3
+    return (2 * done_pieces(tick - jnp.where(tick < LATE, LAG, 1))) // 3
 
 
 def stretch_of(y, core, c):
-    hop = c + 1
-    forward = lax.rem(y + hop, 4)
-    backward = lax.rem(y + 3 * hop, 4)
-    return 2 * jnp.where(core == 0, forward, backward) + c // 4
+    pair = c // 2
+    hop = jnp.where(pair == 0, 2, jnp.where(pair == 3, 0, jnp.where((pair == 1) == (core == 0), 1, 3)))
+    return 2 * lax.rem(y + hop, NY) + lax.rem(c, 2)
 
 
 def kernel(
@@ -131,7 +127,7 @@
 
         return carry
 
-    lax.fori_loop(0, PIECES, distribute, 0)
+    lax.fori_loop(0, EARLY, distribute, 0)
 
     @pl.when(home)
     def _():
@@ -148,6 +144,7 @@
             remote(up_ref.at[k], up_a.at[1, :, k], s_far.at[0], device(x_far, y, z, k))
             remote(up_ref.at[3 - k], up_b.at[1, k], s_far.at[1], device(x_far, y, z, k))
 
+    lax.fori_loop(EARLY, PIECES, distribute, 0)
     local(mom_ref, mom, s_in.at[0])
     local(we_ref, we, s_in.at[1])
     local(se_ref, se, s_in.at[2])
@@ -206,7 +203,7 @@
                 work[rows] = value
                 return total + value * value
 
-            total = lax.fori_loop(0, PIECE // STEP, add, total)
+            total = lax.fori_loop(0, PIECE // STEP, add, total, unroll=True)
         scale, wide = scale_of(total)
         inverse = 1.0 / (LINEAR_SPAN * wide)
         lev[c, pl.ds(SIDE, HEAD)] = jnp.broadcast_to(scale, (HEAD, SIDE))
@@ -219,7 +216,7 @@
             nwe[c, rows] = (value - wide * level.astype(jnp.float32)).astype(jnp.bfloat16)
             return carry
 
-        lax.fori_loop(0, SIDE // STEP, code, 0)
+        lax.fori_loop(0, SIDE // STEP, code, 0, unroll=True)
         mine = at == grp
 
         @pl.when(mine)
@@ -247,7 +244,7 @@
             work[rows] = value
             return total + value * value
 
-        total = lax.fori_loop(0, SIDE // STEP, add, jnp.zeros((STEP, SIDE), jnp.float32))
+        total = lax.fori_loop(0, SIDE // STEP, add, jnp.zeros((STEP, SIDE), jnp.float32), unroll=True)
         scale, wide = scale_of(total)
         inverse = 1.0 / (LINEAR_SPAN * wide)
 
@@ -260,7 +257,7 @@
             nse[rows] = value - decoded
             return carry
 
-        lax.fori_loop(0, SIDE // STEP, code, 0)
+        lax.fori_loop(0, SIDE // STEP, code, 0, unroll=True)
         block = nm.at[grp]
         remote(block, block, s_nm.at[grp], device(x, y_up, z, j))
         remote(block, block, s_nm.at[grp], device(x, y_down, z, j))
@@ -290,69 +287,92 @@
             wait(nm.at[at], s_nm.at[at])
             local(nm.at[at], nm_out.at[at], s_out.at[1])
 
-    def tick(t, carry):
-        def stage(s):
-            i = t - s
-            return i, (i >= 0) & (i < PIECES)
-
-        i0, on = stage(0)
-
-        @pl.when(on)
-        def _():
-            i = i0
-            wait(tok_a.at[i, z, q], s_dist.at[i, 0])
+    def drain_levels(c, carry):
+        @pl.when(stretch_of(y, j, c) != grp)
+        def _():
+            wait(lev.at[c], s_send)
+
+        return carry
+
+    def drain(i, carry):
+        wait(tok_a.at[i], s_send)
+        wait(tok_b.at[i, 0], s_send)
+        wait(tok_b.at[i, 1, pl.ds(0, 6)], s_send)
+        wait(sent_far.at[i], s_send)
+
+        @pl.when(jnp.logical_not(home))
+        def _():
+            wait(sent_own.at[i], s_send)
+            wait(tok_a.at[i, 0], s_send)
+
+        @pl.when(home)
+        def _():
+            wait(tok_a.at[i, 0, 0], s_send)
+
+        return carry
+
+    def drain_gather():
+        lax.fori_loop(0, PIECES, drain, 0)
+        wait(up_ref, s_send)
+        wait(up_a.at[1, :, 0], s_send)
+        wait(up_b.at[1, 0], s_send)
+        lax.fori_loop(0, GROUPS, drain_levels, 0)
+
+    def stage(s, i, carry):
+        if s == 0:
             block = tok_a.at[i, z, q]
+            wait(block, s_dist.at[i, 0])
             remote(block, block, s_ax.at[i], inner)
-            wait(tok_b.at[i, q, z], s_dist.at[i, 1])
             block = tok_b.at[i, q, z]
+            wait(block, s_dist.at[i, 1])
             remote(block, block, s_bz.at[i, 0, 0], above)
             remote(block, block, s_bz.at[i, 0, 1], below)
             remote(block, block, s_bx.at[i], inner)
-
-        for s in range(1, 6):
-            i_s, on = stage(s)
-
-            @pl.when(on)
-            def _(i=i_s, s=s):
-                if s == 1:
-                    wait(tok_a.at[i, z, 1 - q], s_ax.at[i])
-                    block = tok_a.at[i, z]
-                    remote(block, block, s_az.at[i, 0, 0], above)
-                    remote(block, block, s_az.at[i, 0, 1], below)
-                elif s <= 3:
-                    for way, sign, target in ((0, -1, above), (1, 1, below)):
-                        block = tok_a.at[i, z_at(sign * (s - 1))]
-                        wait(block, s_az.at[i, s - 2, way])
-                        remote(block, block, s_az.at[i, s - 1, way], target)
-                elif s == 4:
-                    for way, sign, target in ((0, -1, above), (1, 1, below)):
-                        block = tok_a.at[i, z_at(sign * 3)]
-                        wait(block, s_az.at[i, 2, way])
-                        part = tok_a.at[i, z_at(sign * 3), way]
-                        remote(part, part, s_az.at[i, 3, way], target)
-                else:
-                    for way in range(2):
-                        wait(tok_a.at[i, z_at(4), way], s_az.at[i, 3, way])
-                if s <= 2:
-                    for way, sign, target in ((0, -1, above), (1, 1, below)):
-                        block = tok_b.at[i, q, z_at(sign * s)]
-                        wait(block, s_bz.at[i, s - 1, way])
-                        remote(block, block, s_bz.at[i, s, way], target)
-                        remote(block, block, s_bx.at[i], inner)
-                elif s == 3:
-                    for way, sign, target in ((0, -1, above), (1, 1, below)):
-                        block = tok_b.at[i, q, z_at(sign * 3)]
-                        wait(block, s_bz.at[i, 2, way])
-                        part = tok_b.at[i, q, z_at(sign * 3), pl.ds(32 * way, 32)]
-                        remote(part, part, s_bz.at[i, 3, way], target)
-                        remote(block, block, s_bx.at[i], inner)
-                elif s == 4:
-                    for way in range(2):
-                        wait(tok_b.at[i, q, z_at(4), pl.ds(32 * way, 32)], s_bz.at[i, 3, way])
-                    block = tok_b.at[i, q, z_at(4)]
+        else:
+            if s == 1:
+                wait(tok_a.at[i, z, 1 - q], s_ax.at[i])
+                block = tok_a.at[i, z]
+                remote(block, block, s_az.at[i, 0, 0], above)
+                remote(block, block, s_az.at[i, 0, 1], below)
+            elif s <= 3:
+                for way, sign, target in ((0, -1, above), (1, 1, below)):
+                    block = tok_a.at[i, z_at(sign * (s - 1))]
+                    wait(block, s_az.at[i, s - 2, way])
+                    remote(block, block, s_az.at[i, s - 1, way], target)
+            elif s == 4:
+                for way, sign, target in ((0, -1, above), (1, 1, below)):
+                    block = tok_a.at[i, z_at(sign * 3)]
+                    wait(block, s_az.at[i, 2, way])
+                    part = tok_a.at[i, z_at(sign * 3), way]
+                    remote(part, part, s_az.at[i, 3, way], target)
+            else:
+                for way in range(2):
+                    wait(tok_a.at[i, z_at(4), way], s_az.at[i, 3, way])
+            if s <= 2:
+                for way, sign, target in ((0, -1, above), (1, 1, below)):
+                    block = tok_b.at[i, q, z_at(sign * s)]
+                    wait(block, s_bz.at[i, s - 1, way])
+                    remote(block, block, s_bz.at[i, s, way], target)
                     remote(block, block, s_bx.at[i], inner)
-                else:
-                    wait(tok_b.at[i, 1 - q], s_bx.at[i])
+            elif s == 3:
+                for way, sign, target in ((0, -1, above), (1, 1, below)):
+                    block = tok_b.at[i, q, z_at(sign * 3)]
+                    wait(block, s_bz.at[i, 2, way])
+                    part = tok_b.at[i, q, z_at(sign * 3), pl.ds(32 * way, 32)]
+                    remote(part, part, s_bz.at[i, 3, way], target)
+                    remote(block, block, s_bx.at[i], inner)
+            elif s == 4:
+                for way in range(2):
+                    wait(tok_b.at[i, q, z_at(4), pl.ds(32 * way, 32)], s_bz.at[i, 3, way])
+                block = tok_b.at[i, q, z_at(4)]
+                remote(block, block, s_bx.at[i], inner)
+            else:
+                wait(tok_b.at[i, 1 - q], s_bx.at[i])
+        return carry
+
+    def tick(t, carry):
+        for s in range(6):
+            lax.fori_loop(entered(t - s - 1), entered(t - s), functools.partial(stage, s), 0)
 
         @pl.when(t == RELAY)
         def _():
@@ -374,14 +394,15 @@
             wait(we, s_in.at[1])
             wait(se, s_in.at[2])
 
-        lax.fori_loop(traced_pieces(t - 1), traced_pieces(t), matmul, 0)
-        lax.fori_loop(traced_stretches(t - 1), traced_stretches(t), compress, 0)
-
-        pl.when(t == jnp.where(j == 0, OWN_0, OWN_1))(own)
-        pl.when(t == jnp.where(j == 0, OWN_0, OWN_1) + 1)(spread_near)
-        pl.when(t == jnp.where(j == 0, OWN_0, OWN_1) + 2)(spread_far)
-
-        @pl.when(t == jnp.where(j == 0, OWN_1, OWN_0) + 3)
+        lax.fori_loop(done_pieces(t - 1), done_pieces(t), matmul, 0)
+        lax.fori_loop(done_stretches(t - 1), done_stretches(t), compress, 0)
+
+        pl.when(t == jnp.where(j == 0, OWN[0], OWN[1]))(own)
+        pl.when(t == DRAIN)(drain_gather)
+        pl.when(t == jnp.where(j == 0, NEAR[0], NEAR[1]))(spread_near)
+        pl.when(t == jnp.where(j == 0, FAR[0], FAR[1]))(spread_far)
+
+        @pl.when(t == jnp.where(j == 0, TAKE[1], TAKE[0]))
         def _():
             take(1 - j)
 
@@ -389,44 +410,20 @@
 
     lax.fori_loop(0, TICKS, tick, 0)
 
-    for i in range(PIECES):
-        pass
-
-    def drain(i, carry):
-        wait(tok_a.at[i], s_send)
-        wait(tok_b.at[i, 0], s_send)
-        wait(tok_b.at[i, 1, pl.ds(0, 6)], s_send)
-        wait(sent_far.at[i], s_send)
-
-        @pl.when(jnp.logical_not(home))
-        def _():
-            wait(sent_own.at[i], s_send)
-            wait(tok_a.at[i, 0], s_send)
-
-        @pl.when(home)
-        def _():
-            wait(tok_a.at[i, 0, 0], s_send)
-
-        return carry
-
-    lax.fori_loop(0, PIECES, drain, 0)
-    wait(up_ref, s_send)
-    wait(up_a.at[1, :, 0], s_send)
-    wait(up_b.at[1, 0], s_send)
-
-    def drain_levels(c, carry):
-        @pl.when(stretch_of(y, j, c) != grp)
-        def _():
-            wait(lev.at[c], s_send)
-
-        return carry
-
-    lax.fori_loop(0, GROUPS, drain_levels, 0)
     for _ in range(7):
         wait(nm.at[0], s_send)
     wait(nwe, s_out.at[0])
     wait(nm, s_out.at[1])
     wait(nse, s_out.at[2])
+
+
+def tidy(nm_ref, nwe_ref, nse_ref, nm_out, nwe_out, nse_out, sems):
+    pairs = ((nwe_ref, nwe_out), (nm_ref, nm_out), (nse_ref, nse_out))
+    copies = [pltpu.make_async_copy(src, dst, sems.at[n]) for n, (src, dst) in enumerate(pairs)]
+    for copy in copies:
+        copy.start()
+    for copy in copies:
+        copy.wait()
 
 
 def body(tokens, upstream, momentum, worker_error, server_error):
@@ -478,7 +475,7 @@
         ],
         name="compressed_step",
         compiler_params=pltpu.CompilerParams(
-            collective_id=0, has_side_effects=True, vmem_limit_bytes=48 * 1024 * 1024
+            collective_id=0, has_side_effects=True, vmem_limit_bytes=60 * 1024 * 1024
         ),
     )(
         tokens[0],
@@ -487,6 +484,18 @@
         worker_error[0].reshape(stretches),
         server_error,
     )
+    new_momentum, new_worker_error, new_server_error = pl.pallas_call(
+        tidy,
+        out_shape=(
+            jax.ShapeDtypeStruct(stretches, bf16),
+            jax.ShapeDtypeStruct(stretches, bf16),
+            jax.ShapeDtypeStruct((SIDE, SIDE), f32),
+        ),
+        in_specs=[pl.BlockSpec(memory_space=pltpu.VMEM)] * 3,
+        out_specs=[anywhere] * 3,
+        scratch_shapes=[dma((3,))],
+        name="tidy",
+    )(new_momentum, new_worker_error, new_server_error)
     return (
         new_momentum.reshape(GROUPS * SIDE, SIDE),
         new_worker_error.reshape(1, GROUPS * SIDE, SIDE),

time: 113 us -> 96 us (0.85)
  Pallas kernels: 104 us -> 95.2 us
  local copies, waits for them, and re-layouts: 8.19 us -> 0 us
    pallas_call x1, Pallas kernels: 104 us -> 90.4 us  [body(): pl.pallas_call(kernel, out_shape=(jax.ShapeDtypeStruct(stretches, bf16),...]
    unnamed x11 -> x0, local copies, waits for them, and re-layouts: 8.19 us -> none
    pallas_call x0 -> x1, Pallas kernels: none -> 4.88 us  [body(): pl.pallas_call(tidy, out_shape=(jax.ShapeDtypeStruct(stretches, bf16), ja...]
where the time goes in v2:
time: 96 us; the launch traced here: 95.9 us
  Pallas kernels  95.2 us (99%)
    pallas_call x1, Pallas kernels, body(): pl.pallas_call(kernel, out_shape=(jax.ShapeDtypeStruct(stretches, bf16),...  90.4 us
    pallas_call x1, Pallas kernels, body(): pl.pallas_call(tidy, out_shape=(jax.ShapeDtypeStruct(stretches, bf16), ja...  4.88 us

profile of v2, /device:TPU:1, one launch (start us, length us, event | category | flops | bytes accessed | tf_op | source)
XLA Modules:
  0.0 95.9 jit_solution(7397827937627729512)
XLA Ops:
  0.6 90.4 %compressed_step.1 = (bf16[8,384,384]{2,1,0:T(8,128)(2,1)}, bf16[8,384,384]{2,1,0:T(8,128)(2,1)}, f32[384,384]{1,0:T(8,128)}) custom-call(bf16[64,3072]{1,0:T(8,128)(2,1)} %bitcast.9, bf16[4,8,64,384]{3,2,1,0:T(8,128)(2,1)} %bitcast.8, bf16[8,384,384]{2,1,0:T(8,128)(2,1)} %bitcast.6, bf16[8,384,384]{2,1,0:T(8,128)(2,1)} %bitcast.7, f32[384,384]{1,0:T(8,128)} %se_ref.1), custom_call_target="tpu_custom_call" | custom-call | tf_op jit(solution)/shard_map/compressed_step/pallas_call | solution.py:434
  91.0 4.9 %tidy.1 = (bf16[8,384,384]{2,1,0:T(8,128)(2,1)}, bf16[8,384,384]{2,1,0:T(8,128)(2,1)}, f32[384,384]{1,0:T(8,128)}) custom-call(bf16[8,384,384]{2,1,0:T(8,128)(2,1)} %get-tuple-element.9.nm_ref, bf16[8,384,384]{2,1,0:T(8,128)(2,1)} %get-tuple-element.10.nwe_ref, f32[384,384]{1,0:T(8,128)} %get-tuple-element.11.nse_ref), custom_call_target="tpu_custom_call" | custom-call | tf_op jit(solution)/shard_map/tidy/pallas_call | solution.py:487

commit v3 on v2

--- a/solution.py
+++ b/solution.py
@@ -26,13 +26,15 @@
 FIRST_MM = 7
 RELAY = 6
 LAG = 2
-LATE = 16
+LATE = 20
 OWN = (16, 17)
 NEAR = (17, 18)
 FAR = (18, 19)
 TAKE = (19, 20)
 TICKS = 21
 DRAIN = 17
+UP_AT = 3
+LOAD_AT = 5
 EARLY = 7
 
 
@@ -129,15 +131,6 @@
 
     lax.fori_loop(0, EARLY, distribute, 0)
 
-    @pl.when(home)
-    def _():
-        for k in range(2):
-            local(up_ref.at[k], up_a.at[0, :, k], s_up.at[k])
-            local(up_ref.at[3 - k], up_b.at[0, k], s_up.at[2 + k])
-        for k in range(2):
-            remote(up_ref.at[k], up_a.at[0, :, k], s_up.at[k], sibling)
-            remote(up_ref.at[3 - k], up_b.at[0, k], s_up.at[2 + k], sibling)
-
     @pl.when(jnp.logical_not(home))
     def _():
         for k in range(2):
@@ -145,9 +138,6 @@
             remote(up_ref.at[3 - k], up_b.at[1, k], s_far.at[1], device(x_far, y, z, k))
 
     lax.fori_loop(EARLY, PIECES, distribute, 0)
-    local(mom_ref, mom, s_in.at[0])
-    local(we_ref, we, s_in.at[1])
-    local(se_ref, se, s_in.at[2])
 
     z_at = lambda d: lax.rem(z + d + NZ, NZ)
 
@@ -374,6 +364,21 @@
         for s in range(6):
             lax.fori_loop(entered(t - s - 1), entered(t - s), functools.partial(stage, s), 0)
 
+        @pl.when(home & (t == UP_AT))
+        def _():
+            for k in range(2):
+                local(up_ref.at[k], up_a.at[0, :, k], s_up.at[k])
+                local(up_ref.at[3 - k], up_b.at[0, k], s_up.at[2 + k])
+            for k in range(2):
+                remote(up_ref.at[k], up_a.at[0, :, k], s_up.at[k], sibling)
+                remote(up_ref.at[3 - k], up_b.at[0, k], s_up.at[2 + k], sibling)
+
+        @pl.when(t == LOAD_AT)
+        def _():
+            local(mom_ref, mom, s_in.at[0])
+            local(we_ref, we, s_in.at[1])
+            local(se_ref, se, s_in.at[2])
+
         @pl.when(t == RELAY)
         def _():
             block = up_a.at[1, :, j]
@@ -434,9 +439,9 @@
     new_momentum, new_worker_error, new_server_error = pl.pallas_call(
         kernel,
         out_shape=(
-            jax.ShapeDtypeStruct(stretches, bf16),
-            jax.ShapeDtypeStruct(stretches, bf16),
-            jax.ShapeDtypeStruct((SIDE, SIDE), f32),
+            pltpu.VMEM(stretches, bf16),
+            pltpu.VMEM(stretches, bf16),
+            pltpu.VMEM((SIDE, SIDE), f32),
         ),
         in_specs=[anywhere] * 5,
         out_specs=[anywhere] * 3,
@@ -475,14 +480,19 @@
         ],
         name="compressed_step",
         compiler_params=pltpu.CompilerParams(
-            collective_id=0, has_side_effects=True, vmem_limit_bytes=60 * 1024 * 1024
+            collective_id=0, has_side_effects=True, vmem_limit_bytes=36 * 1024 * 1024
         ),
     )(
-        tokens[0],
-        upstream[0].reshape(NX, NZ, ROWS, SIDE),
-        momentum.reshape(stretches),
-        worker_error[0].reshape(stretches),
-        server_error,
+        *[
+            pltpu.with_memory_space_constraint(value, pltpu.HBM)
+            for value in (
+                tokens[0],
+                upstream[0].reshape(NX, NZ, ROWS, SIDE),
+                momentum.reshape(stretches),
+                worker_error[0].reshape(stretches),
+                server_error,
+            )
+        ]
     )
     new_momentum, new_worker_error, new_server_error = pl.pallas_call(
         tidy,
@@ -491,11 +501,12 @@
             jax.ShapeDtypeStruct(stretches, bf16),
             jax.ShapeDtypeStruct((SIDE, SIDE), f32),
         ),
-        in_specs=[pl.BlockSpec(memory_space=pltpu.VMEM)] * 3,
+        in_specs=[anywhere] * 3,
         out_specs=[anywhere] * 3,
         scratch_shapes=[dma((3,))],
         name="tidy",
-    )(new_momentum, new_worker_error, new_server_error)
+        compiler_params=pltpu.CompilerParams(vmem_limit_bytes=1024 * 1024),
+    )(*[pltpu.with_memory_space_constraint(value, pltpu.VMEM) for value in (new_momentum, new_worker_error, new_server_error)])
     return (
         new_momentum.reshape(GROUPS * SIDE, SIDE),
         new_worker_error.reshape(1, GROUPS * SIDE, SIDE),

time: 96 us -> 93.5 us (0.974)
  Pallas kernels: 95.2 us -> 92.7 us
    pallas_call x1, Pallas kernels: 4.88 us -> 2.4 us  [body(): pl.pallas_call(tidy, out_shape=(jax.ShapeDtypeStruct(stretches, bf16), ja...]
where the time goes in v3:
time: 93.5 us; the launch traced here: 93.3 us
  Pallas kernels  92.7 us (99%)
    pallas_call x1, Pallas kernels, body(): pl.pallas_call(kernel, out_shape=(pltpu.VMEM(stretches, bf16), pltpu.VMEM...  90.3 us
    pallas_call x1, Pallas kernels, body(): pl.pallas_call(tidy, out_shape=(jax.ShapeDtypeStruct(stretches, bf16), ja...  2.4 us

profile of v3, /device:TPU:1, one launch (start us, length us, event | category | flops | bytes accessed | tf_op | source)
XLA Modules:
  0.0 93.3 jit_solution(6816378030108016073)
XLA Ops:
  0.6 90.3 %compressed_step.1 = (bf16[8,384,384]{2,1,0:T(8,128)(2,1)S(1)}, bf16[8,384,384]{2,1,0:T(8,128)(2,1)S(1)}, f32[384,384]{1,0:T(8,128)S(1)}) custom-call(bf16[64,3072]{1,0:T(8,128)(2,1)} %bitcast.9, bf16[4,8,64,384]{3,2,1,0:T(8,128)(2,1)} %bitcast.8, bf16[8,384,384]{2,1,0:T(8,128)(2,1)} %bitcast.6, bf16[8,384,384]{2,1,0:T(8,128)(2,1)} %bitcast.7, f32[384,384]{1,0:T(8,128)} %se_ref.1), custom_call_target="tpu_custom_call" | custom-call | tf_op jit(solution)/shard_map/compressed_step/pallas_call | solution.py:439
  90.9 2.4 %tidy.1 = (bf16[8,384,384]{2,1,0:T(8,128)(2,1)}, bf16[8,384,384]{2,1,0:T(8,128)(2,1)}, f32[384,384]{1,0:T(8,128)}) custom-call(bf16[8,384,384]{2,1,0:T(8,128)(2,1)S(1)} %get-tuple-element.9.nm_ref, bf16[8,384,384]{2,1,0:T(8,128)(2,1)S(1)} %get-tuple-element.10.nwe_ref, f32[384,384]{1,0:T(8,128)S(1)} %get-tuple-element.11.nse_ref), custom_call_target="tpu_custom_call" | custom-call | tf_op jit(solution)/shard_map/tidy/pallas_call | solution.py:497

commit v4 on v3

--- a/solution.py
+++ b/solution.py
@@ -23,8 +23,8 @@
 HALF = SIDE // 2
 
 AHEAD = 1
-FIRST_MM = 7
-RELAY = 6
+FIRST_MM = 6
+RELAY = 5
 LAG = 2
 LATE = 20
 OWN = (16, 17)

time: 93.5 us -> 91.2 us (0.975)
  Pallas kernels: 92.7 us -> 90.4 us
    pallas_call x1, Pallas kernels: 90.3 us -> 88 us  [body(): pl.pallas_call(kernel, out_shape=(pltpu.VMEM(stretches, bf16), pltpu.VMEM...]
where the time goes in v4:
time: 91.2 us; the launch traced here: 91.1 us
  Pallas kernels  90.4 us (99%)
    pallas_call x1, Pallas kernels, body(): pl.pallas_call(kernel, out_shape=(pltpu.VMEM(stretches, bf16), pltpu.VMEM...  88 us
    pallas_call x1, Pallas kernels, body(): pl.pallas_call(tidy, out_shape=(jax.ShapeDtypeStruct(stretches, bf16), ja...  2.4 us

profile of v4, /device:TPU:1, one launch (start us, length us, event | category | flops | bytes accessed | tf_op | source)
XLA Modules:
  0.0 91.1 jit_solution(13483706403125115235)
XLA Ops:
  0.6 88.0 %compressed_step.1 = (bf16[8,384,384]{2,1,0:T(8,128)(2,1)S(1)}, bf16[8,384,384]{2,1,0:T(8,128)(2,1)S(1)}, f32[384,384]{1,0:T(8,128)S(1)}) custom-call(bf16[64,3072]{1,0:T(8,128)(2,1)} %bitcast.9, bf16[4,8,64,384]{3,2,1,0:T(8,128)(2,1)} %bitcast.8, bf16[8,384,384]{2,1,0:T(8,128)(2,1)} %bitcast.6, bf16[8,384,384]{2,1,0:T(8,128)(2,1)} %bitcast.7, f32[384,384]{1,0:T(8,128)} %se_ref.1), custom_call_target="tpu_custom_call" | custom-call | tf_op jit(solution)/shard_map/compressed_step/pallas_call | solution.py:439
  88.7 2.4 %tidy.1 = (bf16[8,384,384]{2,1,0:T(8,128)(2,1)}, bf16[8,384,384]{2,1,0:T(8,128)(2,1)}, f32[384,384]{1,0:T(8,128)}) custom-call(bf16[8,384,384]{2,1,0:T(8,128)(2,1)S(1)} %get-tuple-element.9.nm_ref, bf16[8,384,384]{2,1,0:T(8,128)(2,1)S(1)} %get-tuple-element.10.nwe_ref, f32[384,384]{1,0:T(8,128)S(1)} %get-tuple-element.11.nse_ref), custom_call_target="tpu_custom_call" | custom-call | tf_op jit(solution)/shard_map/tidy/pallas_call | solution.py:497
